TPU v7x, 512 devices: a whole 4x4x16 slice. The times are simulated.
512 devices in a mesh: section: 32 (over z, core), tensor: 8 (over x, y_lo), replica: 2 (over y_hi).
Axes of the slice: x: 4, y: 4 (y_hi: 2, y_lo: 2; y = y_hi * 2 + y_lo), z: 16, core: 2. Of those that a mesh axis runs over, the one named last changes fastest.
Arguments:
- pool_inputs: bfloat16 [32, 256, 2, 1408], P('section', 'replica', None, 'tensor'), may hold values from -6 to 6
- pool_mixed: bfloat16 [32, 256, 1408], P('section', 'replica'), may hold values from -6 to 6
- crop_ids: int32 [32, 8, 128], P('section', 'replica'), may hold values from 0 to 127
- incoming: bfloat16 [32, 256, 1408], P('section', 'replica', 'tensor'), may hold values from -6 to 6
- loss_grads: bfloat16 [3, 256, 1408], P(None, 'replica', 'tensor'), may hold values from -6 to 6
- w_proj: bfloat16 [32, 2, 1408, 1408], P('section', None, ('tensor', 'replica')), may hold values from -0.109375 to 0.109375
- w_up: bfloat16 [32, 1408, 3072], P('section', None, ('tensor', 'replica')), may hold values from -0.15625 to 0.15625
- w_down: bfloat16 [32, 3072, 1408], P('section', ('tensor', 'replica')), may hold values from -0.109375 to 0.109375
Outputs:
- grad_proj: bfloat16 [32, 2, 1408, 1408], P('section', None, ('tensor', 'replica'))
- grad_up: bfloat16 [32, 1408, 3072], P('section', None, ('tensor', 'replica'))
- grad_down: bfloat16 [32, 3072, 1408], P('section', ('tensor', 'replica'))
- outgoing: bfloat16 [32, 256, 2, 1408], P('section', 'replica', None, 'tensor')
All inputs are finite; a program needn't handle non-finite values.
Results may differ from a plain program's by a relative error of at most 0.02.
Values may be sent and summed in bfloat16 or wider, within the bound.
No kernel may reach another device: no remote copies, remote signals or barrier semaphores. Data moves between devices by JAX's collectives and lax.ppermute only.
A program may use at most 64 MiB of HBM per device.

v0:
```python
import jax
import jax.numpy as jnp
from jax import lax
from jax.sharding import PartitionSpec as P

gelu_scale = 0.7978845608
gelu_cubic = 0.044715


def from_partner(value, axis, bit):
    mask = 2**bit
    pairs = [(source, source ^ mask) for source in range(lax.axis_size(axis))]
    return lax.ppermute(value, axis, pairs)


def shifted(x, axis, by):
    devices = lax.axis_size(axis)
    pairs = [(i, i + by) for i in range(devices) if 0 <= i + by < devices]
    return lax.ppermute(x, axis, pairs)


def gelu_pair(pre_gelu):
    inner = gelu_scale * (pre_gelu + gelu_cubic * pre_gelu * pre_gelu * pre_gelu)
    tanh_part = jnp.tanh(inner)
    gelu_value = 0.5 * pre_gelu * (1.0 + tanh_part)
    gelu_slope = 0.5 * (1.0 + tanh_part) + 0.5 * pre_gelu * (
        1.0 - tanh_part * tanh_part
    ) * gelu_scale * (1.0 + 3.0 * gelu_cubic * pre_gelu * pre_gelu)
    return (gelu_value, gelu_slope)


def reflect(block, section_count):
    for bit_number in range(section_count.bit_length() - 1):
        block = from_partner(block, "section", bit_number)
    return block


def body(pool_inputs, pool_mixed, crop_ids, incoming, loss_grads, w_proj, w_up, w_down):
    section_index = lax.axis_index("section")
    section_count = lax.axis_size("section")
    proj_full, up_full, down_full = (
        lax.all_gather(w_proj, "replica", axis=2, tiled=True),
        lax.all_gather(w_up, "replica", axis=2, tiled=True),
        lax.all_gather(w_down, "replica", axis=1, tiled=True),
    )
    proj_local = proj_full[0]
    up_local = up_full[0]
    down_local = down_full[0]
    seed_full, loss_full = (
        lax.all_gather(incoming, "tensor", axis=2, tiled=True),
        lax.all_gather(loss_grads, "tensor", axis=2, tiled=True),
    )
    encoder = section_index < section_count // 2
    decoder_flag = jnp.where(encoder, 0.0, 1.0).astype(jnp.bfloat16)
    skip_mask = jnp.stack([jnp.ones((), jnp.bfloat16), decoder_flag])[None, :, None]
    encoder_weight = jnp.where(encoder, 1.0, 0.0).astype(jnp.float32)
    is_top = section_index == section_count - 1
    tick_count = crop_ids.shape[1]
    upstream = seed_full[0]
    kept_inputs, kept_mixed, kept_active, kept_hidden, kept_grads, kept_upstream = (
        [],
        [],
        [],
        [],
        [],
        [],
    )
    input_grad = None
    for tick_index in range(tick_count):
        picked_rows = crop_ids[0, tick_index]
        inputs = pool_inputs[0][picked_rows] * skip_mask
        mixed_rows = pool_mixed[0][picked_rows]
        pre_gelu = jnp.dot(mixed_rows, up_local, preferred_element_type=jnp.float32)
        gelu_value, gelu_slope = gelu_pair(pre_gelu)
        activated = gelu_value.astype(jnp.bfloat16)
        back_act = jnp.einsum("md,fd->mf", upstream, down_local, preferred_element_type=jnp.float32)
        back_hidden = (back_act * gelu_slope).astype(jnp.bfloat16)
        partial_back = jnp.einsum(
            "mf,df->md", back_hidden, up_local, preferred_element_type=jnp.float32
        )
        back_mixed = upstream.astype(jnp.float32) + lax.psum(partial_back, "tensor")
        mixed_grad = back_mixed.astype(jnp.bfloat16)
        input_grad = jnp.einsum(
            "mj,kij->mki", mixed_grad, proj_local, preferred_element_type=jnp.float32
        ).astype(jnp.bfloat16)
        kept_inputs.append(inputs)
        kept_mixed.append(mixed_rows)
        kept_active.append(activated)
        kept_hidden.append(back_hidden)
        kept_grads.append(mixed_grad)
        kept_upstream.append(upstream)
        if tick_index + 1 < tick_count:
            payload = lax.all_gather(input_grad, "tensor", axis=2, tiled=True)
            from_above = shifted(payload[:, 0], "section", -1)
            mirrored = reflect(payload[:, 1], section_count)
            summed = (
                from_above.astype(jnp.float32) + encoder_weight * mirrored.astype(jnp.float32)
            ).astype(jnp.bfloat16)
            upstream = jnp.where(is_top, loss_full[tick_index], summed)
    all_inputs = jnp.concatenate(kept_inputs, axis=0)
    all_mixed = jnp.concatenate(kept_mixed, axis=0)
    all_active = jnp.concatenate(kept_active, axis=0)
    all_hidden = jnp.concatenate(kept_hidden, axis=0)
    all_grads = jnp.concatenate(kept_grads, axis=0)
    all_upstream = jnp.concatenate(kept_upstream, axis=0)
    down_total = jnp.einsum(
        "mf,md->fd", all_active, all_upstream, preferred_element_type=jnp.float32
    )
    up_total = jnp.einsum("md,mf->df", all_mixed, all_hidden, preferred_element_type=jnp.float32)
    proj_total = jnp.einsum(
        "mki,mj->kij", all_inputs, all_grads, preferred_element_type=jnp.float32
    )
    reduced = (
        lax.psum_scatter(
            proj_total[None].astype(jnp.bfloat16), "replica", scatter_dimension=2, tiled=True
        ).astype(jnp.float32),
        lax.psum_scatter(
            up_total[None].astype(jnp.bfloat16), "replica", scatter_dimension=2, tiled=True
        ).astype(jnp.float32),
        lax.psum_scatter(
            down_total[None].astype(jnp.bfloat16), "replica", scatter_dimension=1, tiled=True
        ).astype(jnp.float32),
    )
    return (
        reduced[0].astype(jnp.bfloat16),
        reduced[1].astype(jnp.bfloat16),
        reduced[2].astype(jnp.bfloat16),
        input_grad[None],
    )


def solution(mesh):
    in_specs = (
        P("section", "replica", None, "tensor"),
        P("section", "replica", None),
        P("section", "replica", None),
        P("section", "replica", "tensor"),
        P(None, "replica", "tensor"),
        P("section", None, ("tensor", "replica"), None),
        P("section", None, ("tensor", "replica")),
        P("section", ("tensor", "replica"), None),
    )
    out_specs = (
        P("section", None, ("tensor", "replica"), None),
        P("section", None, ("tensor", "replica")),
        P("section", ("tensor", "replica"), None),
        P("section", "replica", None, "tensor"),
    )
    return jax.shard_map(body, mesh=mesh, in_specs=in_specs, out_specs=out_specs, check_vma=False)
```

profile of v0, /device:TPU:1, one launch (start us, length us, event | category | flops | bytes accessed | tf_op | source)
XLA Modules:
  0.0 1007.1 jit_solution(8471942278215179916)
XLA Ops:
  9.7 23.1 %all_gather.24 = bf16[1,128,1408]{1,2,0:T(8,128)(2,1)S(1)} all-gather(bf16[1,128,176]{1,2,0:T(8,128)(2,1)S(1)} %copy-done.36), channel_id=1, replica_groups=mesh['section'=32,'tensor'=8,'replica'=2] {'tensor'}, dimensions={2}, use_global_device_ids=true | all-gather | bytes 405504 | tf_op jit(solution)/shard_map/all_gather | solution.py:50
  32.8 16.5 %all-gather.6.cloned.1.call-done = bf16[1,1408,384]{1,2,0:T(8,128)(2,1)} async-done(((bf16[1,1408,192]{1,2,0:T(8,128)(2,1)}), bf16[1,1408,384]{1,2,0:T(8,128)(2,1)}) %all-gather.6.cloned.1.call-update) | async-done | bytes 1081360 | tf_op jit(solution)/shard_map/all_gather | solution.py:43
  49.3 2.4 multiply_convert_fusion.3
  51.7 33.1 %all-gather.4.cloned.1.call-done = bf16[1,384,1408]{2,1,0:T(8,128)(2,1)} async-done(((bf16[1,192,1408]{2,1,0:T(8,128)(2,1)}), bf16[1,384,1408]{2,1,0:T(8,128)(2,1)}) %all-gather.4.cloned.1.call-update) | async-done | bytes 1081360 | tf_op jit(solution)/shard_map/all_gather | solution.py:44
  84.8 1.7 fusion.23
  89.5 14.4 %all_gather.28 = bf16[1,2,176,1408]{3,2,1,0:T(8,128)(2,1)S(1)} all-gather(bf16[1,2,88,1408]{3,2,1,0:T(8,128)(2,1)S(1)} %copy-done.23), channel_id=1, replica_groups=mesh['section'=32,'tensor'=8,'replica'=2] {'replica'}, dimensions={2}, use_global_device_ids=true | all-gather | bytes 1486848 | tf_op jit(solution)/shard_map/all_gather | solution.py:42
  103.8 70.2 %all-reduce.5.cloned.1.call-done = f32[128,1408]{1,0:T(8,128)} async-done(((f32[128,1408]{1,0:T(8,128)}), f32[128,1408]{1,0:T(8,128)}) %all-reduce.5.cloned.1.call-update) | async-done | bytes 720912 | tf_op jit(solution)/shard_map/psum | solution.py:81
  176.0 23.6 %all_gather.29 = bf16[128,2,1408]{0,1,2:T(2,128)(2,1)S(1)} all-gather(bf16[128,2,176]{0,1,2:T(2,128)(2,1)S(1)} %copy.36), channel_id=1, replica_groups=mesh['section'=32,'tensor'=8,'replica'=2] {'tensor'}, dimensions={2}, use_global_device_ids=true | all-gather | bytes 811008 | tf_op jit(solution)/shard_map/all_gather | solution.py:93
  199.6 1.8 fusion.111
  201.4 2.8 copy.56
  204.3 14.3 %collective-permute-start.1 = (bf16[128,1408]{1,0:T(8,128)(2,1)}, bf16[128,1408]{1,0:T(8,128)(2,1)S(1)}, u32[]{:S(2)}, u32[]{:S(2)}) collective-permute-start(bf16[128,1408]{1,0:T(8,128)(2,1)} %bitcast.141), channel_id=1, source_target_pairs={{0,16},{16,0},{32,48},{48,32},{64,80},{80,64},{96,112},{112,96},{1... | collective-permute-start | bytes 1081352 | tf_op jit(solution)/shard_map/ppermute | solution.py:13
  220.1 3.2 collective-permute-start.2
  223.2 8.4 collective-permute-done.2
  231.7 4.6 collective-permute-start.3
  236.3 16.0 %collective-permute-done.3 = bf16[128,1408]{1,0:T(8,128)(2,1)} collective-permute-done((bf16[128,1408]{1,0:T(8,128)(2,1)}, bf16[128,1408]{1,0:T(8,128)(2,1)}, u32[]{:S(2)}, u32[]{:S(2)}) %collective-permute-start.3) | collective-permute-done | bytes 360480 | tf_op jit(solution)/shard_map/ppermute | solution.py:13
  252.3 7.1 collective-permute-start.4
  259.5 1.7 gather_fusion.5
  261.1 2.2 multiply_convert_fusion.2
  263.3 1.6 copy.55
  265.0 3.7 collective-permute-start
  268.7 22.2 %collective-permute-done.4 = bf16[128,1408]{1,0:T(8,128)(2,1)} collective-permute-done((bf16[128,1408]{1,0:T(8,128)(2,1)}, bf16[128,1408]{1,0:T(8,128)(2,1)}, u32[]{:S(2)}, u32[]{:S(2)}) %collective-permute-start.4) | collective-permute-done | bytes 360480 | tf_op jit(solution)/shard_map/ppermute | solution.py:13
  290.9 18.8 %collective-permute-start.5 = (bf16[128,1408]{1,0:T(8,128)(2,1)}, bf16[128,1408]{1,0:T(8,128)(2,1)}, u32[]{:S(2)}, u32[]{:S(2)}) collective-permute-start(bf16[128,1408]{1,0:T(8,128)(2,1)} %collective-permute-done.4), channel_id=1, source_target_pairs={{0,256},{16,272},{32,288},{48,304},{64,320},{80,336},{96,352},{112... | collective-permute-start | bytes 1081352 | tf_op jit(solution)/shard_map/ppermute | solution.py:13
  309.8 2.1 fusion.108
  312.2 12.0 %collective-permute-done.5 = bf16[128,1408]{1,0:T(8,128)(2,1)} collective-permute-done((bf16[128,1408]{1,0:T(8,128)(2,1)}, bf16[128,1408]{1,0:T(8,128)(2,1)}, u32[]{:S(2)}, u32[]{:S(2)}) %collective-permute-start.5) | collective-permute-done | bytes 360480 | tf_op jit(solution)/shard_map/ppermute | solution.py:13
  327.9 87.2 %all-reduce.7.cloned.1.call-done = f32[128,1408]{1,0:T(8,128)} async-done(((f32[128,1408]{1,0:T(8,128)}), f32[128,1408]{1,0:T(8,128)}) %all-reduce.7.cloned.1.call-update) | async-done | bytes 720912 | tf_op jit(solution)/shard_map/psum | solution.py:81
  417.0 23.3 %all_gather.30 = bf16[128,2,1408]{0,1,2:T(2,128)(2,1)S(1)} all-gather(bf16[128,2,176]{0,1,2:T(2,128)(2,1)S(1)} %copy.40), channel_id=1, replica_groups=mesh['section'=32,'tensor'=8,'replica'=2] {'tensor'}, dimensions={2}, use_global_device_ids=true | all-gather | bytes 811008 | tf_op jit(solution)/shard_map/all_gather | solution.py:93
  440.3 1.8 fusion.110
  442.1 2.8 copy.59
  444.9 13.9 %collective-permute-start.7 = (bf16[128,1408]{1,0:T(8,128)(2,1)}, bf16[128,1408]{1,0:T(8,128)(2,1)S(1)}, u32[]{:S(2)}, u32[]{:S(2)}) collective-permute-start(bf16[128,1408]{1,0:T(8,128)(2,1)} %bitcast.142), channel_id=1, source_target_pairs={{0,16},{16,0},{32,48},{48,32},{64,80},{80,64},{96,112},{112,96},{1... | collective-permute-start | bytes 1081352 | tf_op jit(solution)/shard_map/ppermute | solution.py:13
  460.3 3.0 collective-permute-start.8
  463.3 8.5 collective-permute-done.8
  471.8 4.0 collective-permute-start.9
  475.9 16.0 %collective-permute-done.9 = bf16[128,1408]{1,0:T(8,128)(2,1)} collective-permute-done((bf16[128,1408]{1,0:T(8,128)(2,1)S(1)}, bf16[128,1408]{1,0:T(8,128)(2,1)}, u32[]{:S(2)}, u32[]{:S(2)}) %collective-permute-start.9) | collective-permute-done | bytes 360480 | tf_op jit(solution)/shard_map/ppermute | solution.py:13
  491.9 7.0 collective-permute-start.10
  498.9 1.7 copy.58
  500.6 3.7 collective-permute-start.6
  504.4 26.1 %collective-permute-done.10 = bf16[128,1408]{1,0:T(8,128)(2,1)} collective-permute-done((bf16[128,1408]{1,0:T(8,128)(2,1)}, bf16[128,1408]{1,0:T(8,128)(2,1)}, u32[]{:S(2)}, u32[]{:S(2)}) %collective-permute-start.10) | collective-permute-done | bytes 360480 | tf_op jit(solution)/shard_map/ppermute | solution.py:13
  530.4 18.7 %collective-permute-start.11 = (bf16[128,1408]{1,0:T(8,128)(2,1)}, bf16[128,1408]{1,0:T(8,128)(2,1)}, u32[]{:S(2)}, u32[]{:S(2)}) collective-permute-start(bf16[128,1408]{1,0:T(8,128)(2,1)} %collective-permute-done.10), channel_id=1, source_target_pairs={{0,256},{16,272},{32,288},{48,304},{64,320},{80,336},{96,352},{112... | collective-permute-start | bytes 1081352 | tf_op jit(solution)/shard_map/ppermute | solution.py:13
  551.5 12.0 %collective-permute-done.11 = bf16[128,1408]{1,0:T(8,128)(2,1)} collective-permute-done((bf16[128,1408]{1,0:T(8,128)(2,1)}, bf16[128,1408]{1,0:T(8,128)(2,1)}, u32[]{:S(2)}, u32[]{:S(2)}) %collective-permute-start.11) | collective-permute-done | bytes 360480 | tf_op jit(solution)/shard_map/ppermute | solution.py:13
  566.6 86.3 %all-reduce.9.cloned.1.call-done = f32[128,1408]{1,0:T(8,128)} async-done(((f32[128,1408]{1,0:T(8,128)}), f32[128,1408]{1,0:T(8,128)}) %all-reduce.9.cloned.1.call-update) | async-done | bytes 720912 | tf_op jit(solution)/shard_map/psum | solution.py:81
  654.8 23.3 %all_gather.31 = bf16[128,2,1408]{0,1,2:T(2,128)(2,1)S(1)} all-gather(bf16[128,2,176]{0,1,2:T(2,128)(2,1)S(1)} %copy.44), channel_id=1, replica_groups=mesh['section'=32,'tensor'=8,'replica'=2] {'tensor'}, dimensions={2}, use_global_device_ids=true | all-gather | bytes 811008 | tf_op jit(solution)/shard_map/all_gather | solution.py:93
  678.1 1.8 fusion.109
  679.9 2.8 copy.62
  682.7 13.9 %collective-permute-start.13 = (bf16[128,1408]{1,0:T(8,128)(2,1)}, bf16[128,1408]{1,0:T(8,128)(2,1)S(1)}, u32[]{:S(2)}, u32[]{:S(2)}) collective-permute-start(bf16[128,1408]{1,0:T(8,128)(2,1)} %bitcast.143), channel_id=1, source_target_pairs={{0,16},{16,0},{32,48},{48,32},{64,80},{80,64},{96,112},{112,96},{1... | collective-permute-start | bytes 1081352 | tf_op jit(solution)/shard_map/ppermute | solution.py:13
  698.1 3.0 collective-permute-start.14
  701.1 8.5 collective-permute-done.14
  709.6 4.0 collective-permute-start.15
  713.6 16.0 %collective-permute-done.15 = bf16[128,1408]{1,0:T(8,128)(2,1)} collective-permute-done((bf16[128,1408]{1,0:T(8,128)(2,1)S(1)}, bf16[128,1408]{1,0:T(8,128)(2,1)}, u32[]{:S(2)}, u32[]{:S(2)}) %collective-permute-start.15) | collective-permute-done | bytes 360480 | tf_op jit(solution)/shard_map/ppermute | solution.py:13
  729.7 7.2 collective-permute-start.16
  736.9 1.7 copy.61
  738.6 3.7 collective-permute-start.12
  742.3 25.9 %collective-permute-done.16 = bf16[128,1408]{1,0:T(8,128)(2,1)} collective-permute-done((bf16[128,1408]{1,0:T(8,128)(2,1)}, bf16[128,1408]{1,0:T(8,128)(2,1)}, u32[]{:S(2)}, u32[]{:S(2)}) %collective-permute-start.16) | collective-permute-done | bytes 360480 | tf_op jit(solution)/shard_map/ppermute | solution.py:13
  768.2 18.7 %collective-permute-start.17 = (bf16[128,1408]{1,0:T(8,128)(2,1)}, bf16[128,1408]{1,0:T(8,128)(2,1)}, u32[]{:S(2)}, u32[]{:S(2)}) collective-permute-start(bf16[128,1408]{1,0:T(8,128)(2,1)} %collective-permute-done.16), channel_id=1, source_target_pairs={{0,256},{16,272},{32,288},{48,304},{64,320},{80,336},{96,352},{112... | collective-permute-start | bytes 1081352 | tf_op jit(solution)/shard_map/ppermute | solution.py:13
  789.3 12.0 %collective-permute-done.17 = bf16[128,1408]{1,0:T(8,128)(2,1)} collective-permute-done((bf16[128,1408]{1,0:T(8,128)(2,1)}, bf16[128,1408]{1,0:T(8,128)(2,1)}, u32[]{:S(2)}, u32[]{:S(2)}) %collective-permute-start.17) | collective-permute-done | bytes 360480 | tf_op jit(solution)/shard_map/ppermute | solution.py:13
  805.8 2.2 fusion
  807.9 4.8 copy.50
  812.8 2.7 copy.65
  821.3 1.8 broadcast_multiply_fusion.3
  823.1 68.8 %all-reduce.11.cloned.1.call-done = f32[128,1408]{1,0:T(8,128)} async-done(((f32[128,1408]{1,0:T(8,128)}), f32[128,1408]{1,0:T(8,128)}) %all-reduce.11.cloned.1.call-update) | async-done | bytes 720912 | tf_op jit(solution)/shard_map/psum | solution.py:81
  896.7 3.0 fusion.1
  901.8 29.7 %reduce-scatter.12.cloned.1.call-done = bf16[192,1408]{1,0:T(8,128)(2,1)} async-done(((bf16[384,1408]{1,0:T(8,128)(2,1)}), bf16[192,1408]{1,0:T(8,128)(2,1)}) %reduce-scatter.12.cloned.1.call-update) | async-done | bytes 540688
  931.4 1.6 reshape_bitcast_fusion
  933.9 31.3 %reduce-scatter.10.cloned.1.call-done = bf16[88,2816]{1,0:T(8,128)(2,1)} async-done(((bf16[176,2816]{1,0:T(8,128)(2,1)}), bf16[88,2816]{1,0:T(8,128)(2,1)}) %reduce-scatter.10.cloned.1.call-update) | async-done | bytes 495632
  967.2 33.1 %reduce-scatter.8.cloned.1.call-done = bf16[1,192,1408]{2,1,0:T(8,128)(2,1)} async-done(((bf16[1,384,1408]{2,1,0:T(8,128)(2,1)}), bf16[1,192,1408]{2,1,0:T(8,128)(2,1)}) %reduce-scatter.8.cloned.1.call-update) | async-done | bytes 540688 | tf_op jit(solution)/shard_map/reduce_scatter | solution.py:120
  (160 shorter events, 47.1 us)
Async XLA Ops:
  7.2 1.6 copy-start
  7.2 1.5 copy-start.37
  7.2 42.2 %all-gather.6.cloned.1.call-start = ((), (), s32[]{:S(2)}) async-start(), calls=%async_computation.4 | async-start | bytes 1622016 | tf_op jit(solution)/shard_map/all_gather | solution.py:43
  7.9 76.9 %all-gather.4.cloned.1.call-start = ((), (), s32[]{:S(2)}) async-start(), calls=%async_computation.3 | async-start | bytes 1622016 | tf_op jit(solution)/shard_map/all_gather | solution.py:44
  8.7 165.4 %all-reduce.5.cloned.1.call-start = ((), (), s32[]{:S(2)}) async-start(), calls=%async_computation.5 | async-start | bytes 1441792 | tf_op jit(solution)/shard_map/psum | solution.py:81
  8.8 0.9 copy-start.36
  9.7 76.9 %copy-start.6 = (bf16[128,1408]{1,0:T(8,128)(2,1)}, bf16[128,1408]{1,0:T(8,128)(2,1)S(1)}, u32[]{:S(2)}) copy-start(bf16[128,1408]{1,0:T(8,128)(2,1)S(1)} %gather_fusion.4) | copy-start | bytes 1081348
  51.7 35.5 %copy-start.1 = (bf16[1,1408,384]{1,2,0:T(8,128)(2,1)S(1)}, bf16[1,1408,384]{1,2,0:T(8,128)(2,1)}, u32[]{:S(2)}) copy-start(bf16[1,1408,384]{1,2,0:T(8,128)(2,1)} %all-gather.6.cloned.1.call-done) | copy-start | bytes 3244036
  88.4 1.0 copy-start.23
  88.5 221.3 %all-gather.8.cloned.1.call-start = ((), (), s32[]{:S(2)}) async-start(), calls=%async_computation.6 | async-start | bytes 1216512 | tf_op jit(solution)/shard_map/all_gather | solution.py:51
  89.1 326.0 %all-reduce.7.cloned.1.call-start = ((), (), s32[]{:S(2)}) async-start(), calls=%async_computation.7 | async-start | bytes 1441792 | tf_op jit(solution)/shard_map/psum | solution.py:81
  175.2 0.7 copy-start.4
  204.3 15.8 %collective-permute-start.1 = (bf16[128,1408]{1,0:T(8,128)(2,1)}, bf16[128,1408]{1,0:T(8,128)(2,1)S(1)}, u32[]{:S(2)}, u32[]{:S(2)}) collective-permute-start(bf16[128,1408]{1,0:T(8,128)(2,1)} %bitcast.141), channel_id=1, source_target_pairs={{0,16},{16,0},{32,48},{48,32},{64,80},{80,64},{96,112},{112,96},{1... | collective-permute-start | bytes 1081352 | tf_op jit(solution)/shard_map/ppermute | solution.py:13
  220.1 11.6 %collective-permute-start.2 = (bf16[128,1408]{1,0:T(8,128)(2,1)S(1)}, bf16[128,1408]{1,0:T(8,128)(2,1)}, u32[]{:S(2)}, u32[]{:S(2)}) collective-permute-start(bf16[128,1408]{1,0:T(8,128)(2,1)S(1)} %collective-permute-done.1), channel_id=1, source_target_pairs={{0,32},{16,48},{32,0},{48,16},{64,96},{80,112},{96,64},{112,80},{1... | collective-permute-start | bytes 1081352 | tf_op jit(solution)/shard_map/ppermute | solution.py:13
  231.7 20.6 %collective-permute-start.3 = (bf16[128,1408]{1,0:T(8,128)(2,1)}, bf16[128,1408]{1,0:T(8,128)(2,1)}, u32[]{:S(2)}, u32[]{:S(2)}) collective-permute-start(bf16[128,1408]{1,0:T(8,128)(2,1)} %collective-permute-done.2), channel_id=1, source_target_pairs={{0,64},{16,80},{32,96},{48,112},{64,0},{80,16},{96,32},{112,48},{1... | collective-permute-start | bytes 1081352 | tf_op jit(solution)/shard_map/ppermute | solution.py:13
  252.3 38.6 %collective-permute-start.4 = (bf16[128,1408]{1,0:T(8,128)(2,1)}, bf16[128,1408]{1,0:T(8,128)(2,1)}, u32[]{:S(2)}, u32[]{:S(2)}) collective-permute-start(bf16[128,1408]{1,0:T(8,128)(2,1)} %collective-permute-done.3), channel_id=1, source_target_pairs={{0,128},{16,144},{32,160},{48,176},{64,192},{80,208},{96,224},{112... | collective-permute-start | bytes 1081352 | tf_op jit(solution)/shard_map/ppermute | solution.py:13
  265.0 47.2 %collective-permute-start = (bf16[128,1408]{1,0:T(8,128)(2,1)}, bf16[128,1408]{1,0:T(8,128)(2,1)}, u32[]{:S(2)}, u32[]{:S(2)}) collective-permute-start(bf16[128,1408]{1,0:T(8,128)(2,1)} %bitcast.138), channel_id=1, source_target_pairs={{16,0},{32,16},{48,32},{64,48},{80,64},{96,80},{112,96},{128,112},... | collective-permute-start | bytes 1081352 | tf_op jit(solution)/shard_map/ppermute | solution.py:19
  290.9 33.2 %collective-permute-start.5 = (bf16[128,1408]{1,0:T(8,128)(2,1)}, bf16[128,1408]{1,0:T(8,128)(2,1)}, u32[]{:S(2)}, u32[]{:S(2)}) collective-permute-start(bf16[128,1408]{1,0:T(8,128)(2,1)} %collective-permute-done.4), channel_id=1, source_target_pairs={{0,256},{16,272},{32,288},{48,304},{64,320},{80,336},{96,352},{112... | collective-permute-start | bytes 1081352 | tf_op jit(solution)/shard_map/ppermute | solution.py:13
  312.2 13.3 %copy-start.24 = (f32[128,384]{1,0:T(8,128)S(1)}, f32[128,384]{1,0:T(8,128)}, u32[]{:S(2)}) copy-start(f32[128,384]{1,0:T(8,128)} %get-tuple-element.38) | copy-start | bytes 589828
  312.2 13.3 %copy-start.38 = (bf16[1,384,1408]{2,1,0:T(8,128)(2,1)S(1)}, bf16[1,384,1408]{2,1,0:T(8,128)(2,1)}, u32[]{:S(2)}) copy-start(bf16[1,384,1408]{2,1,0:T(8,128)(2,1)} %all-gather.4.cloned.1.call-done) | copy-start | bytes 3244036
  325.4 89.7 %copy-start.8 = (bf16[128,1408]{1,0:T(8,128)(2,1)}, bf16[128,1408]{1,0:T(8,128)(2,1)S(1)}, u32[]{:S(2)}) copy-start(bf16[128,1408]{1,0:T(8,128)(2,1)S(1)} %fusion.66) | copy-start | bytes 1081348
  327.9 325.0 %all-reduce.9.cloned.1.call-start = ((), (), s32[]{:S(2)}) async-start(), calls=%async_computation.8 | async-start | bytes 1441792 | tf_op jit(solution)/shard_map/psum | solution.py:81
  416.3 0.7 copy-start.10
  444.9 15.4 %collective-permute-start.7 = (bf16[128,1408]{1,0:T(8,128)(2,1)}, bf16[128,1408]{1,0:T(8,128)(2,1)S(1)}, u32[]{:S(2)}, u32[]{:S(2)}) collective-permute-start(bf16[128,1408]{1,0:T(8,128)(2,1)} %bitcast.142), channel_id=1, source_target_pairs={{0,16},{16,0},{32,48},{48,32},{64,80},{80,64},{96,112},{112,96},{1... | collective-permute-start | bytes 1081352 | tf_op jit(solution)/shard_map/ppermute | solution.py:13
  460.3 11.5 %collective-permute-start.8 = (bf16[128,1408]{1,0:T(8,128)(2,1)S(1)}, bf16[128,1408]{1,0:T(8,128)(2,1)S(1)}, u32[]{:S(2)}, u32[]{:S(2)}) collective-permute-start(bf16[128,1408]{1,0:T(8,128)(2,1)S(1)} %collective-permute-done.7), channel_id=1, source_target_pairs={{0,32},{16,48},{32,0},{48,16},{64,96},{80,112},{96,64},{112,80},{1... | collective-permute-start | bytes 1081352 | tf_op jit(solution)/shard_map/ppermute | solution.py:13
  471.8 20.1 %collective-permute-start.9 = (bf16[128,1408]{1,0:T(8,128)(2,1)S(1)}, bf16[128,1408]{1,0:T(8,128)(2,1)}, u32[]{:S(2)}, u32[]{:S(2)}) collective-permute-start(bf16[128,1408]{1,0:T(8,128)(2,1)S(1)} %collective-permute-done.8), channel_id=1, source_target_pairs={{0,64},{16,80},{32,96},{48,112},{64,0},{80,16},{96,32},{112,48},{1... | collective-permute-start | bytes 1081352 | tf_op jit(solution)/shard_map/ppermute | solution.py:13
  491.9 38.5 %collective-permute-start.10 = (bf16[128,1408]{1,0:T(8,128)(2,1)}, bf16[128,1408]{1,0:T(8,128)(2,1)}, u32[]{:S(2)}, u32[]{:S(2)}) collective-permute-start(bf16[128,1408]{1,0:T(8,128)(2,1)} %collective-permute-done.9), channel_id=1, source_target_pairs={{0,128},{16,144},{32,160},{48,176},{64,192},{80,208},{96,224},{112... | collective-permute-start | bytes 1081352 | tf_op jit(solution)/shard_map/ppermute | solution.py:13
  500.6 50.9 %collective-permute-start.6 = (bf16[128,1408]{1,0:T(8,128)(2,1)}, bf16[128,1408]{1,0:T(8,128)(2,1)}, u32[]{:S(2)}, u32[]{:S(2)}) collective-permute-start(bf16[128,1408]{1,0:T(8,128)(2,1)} %bitcast.140), channel_id=1, source_target_pairs={{16,0},{32,16},{48,32},{64,48},{80,64},{96,80},{112,96},{128,112},... | collective-permute-start | bytes 1081352 | tf_op jit(solution)/shard_map/ppermute | solution.py:19
  530.4 33.0 %collective-permute-start.11 = (bf16[128,1408]{1,0:T(8,128)(2,1)}, bf16[128,1408]{1,0:T(8,128)(2,1)}, u32[]{:S(2)}, u32[]{:S(2)}) collective-permute-start(bf16[128,1408]{1,0:T(8,128)(2,1)} %collective-permute-done.10), channel_id=1, source_target_pairs={{0,256},{16,272},{32,288},{48,304},{64,320},{80,336},{96,352},{112... | collective-permute-start | bytes 1081352 | tf_op jit(solution)/shard_map/ppermute | solution.py:13
  550.0 1.2 copy-start.17
  550.0 1.2 copy-start.3
  551.5 13.3 %copy-start.26 = (f32[128,384]{1,0:T(8,128)S(1)}, f32[128,384]{1,0:T(8,128)}, u32[]{:S(2)}) copy-start(f32[128,384]{1,0:T(8,128)} %get-tuple-element.36) | copy-start | bytes 589828
  551.5 13.3 %copy-start.39 = (bf16[1,384,1408]{2,1,0:T(8,128)(2,1)S(1)}, bf16[1,384,1408]{2,1,0:T(8,128)(2,1)}, u32[]{:S(2)}) copy-start(bf16[1,384,1408]{2,1,0:T(8,128)(2,1)} %all-gather.4.cloned.1.call-done) | copy-start | bytes 3244036
  564.8 88.1 %copy-start.13 = (bf16[128,1408]{1,0:T(8,128)(2,1)}, bf16[128,1408]{1,0:T(8,128)(2,1)S(1)}, u32[]{:S(2)}) copy-start(bf16[128,1408]{1,0:T(8,128)(2,1)S(1)} %fusion.67) | copy-start | bytes 1081348
  565.3 1.3 copy-start.29
  566.6 325.3 %all-reduce.11.cloned.1.call-start = ((), (), s32[]{:S(2)}) async-start(), calls=%async_computation.9 | async-start | bytes 1441792 | tf_op jit(solution)/shard_map/psum | solution.py:81
  682.7 15.4 %collective-permute-start.13 = (bf16[128,1408]{1,0:T(8,128)(2,1)}, bf16[128,1408]{1,0:T(8,128)(2,1)S(1)}, u32[]{:S(2)}, u32[]{:S(2)}) collective-permute-start(bf16[128,1408]{1,0:T(8,128)(2,1)} %bitcast.143), channel_id=1, source_target_pairs={{0,16},{16,0},{32,48},{48,32},{64,80},{80,64},{96,112},{112,96},{1... | collective-permute-start | bytes 1081352 | tf_op jit(solution)/shard_map/ppermute | solution.py:13
  698.1 11.5 %collective-permute-start.14 = (bf16[128,1408]{1,0:T(8,128)(2,1)S(1)}, bf16[128,1408]{1,0:T(8,128)(2,1)S(1)}, u32[]{:S(2)}, u32[]{:S(2)}) collective-permute-start(bf16[128,1408]{1,0:T(8,128)(2,1)S(1)} %collective-permute-done.13), channel_id=1, source_target_pairs={{0,32},{16,48},{32,0},{48,16},{64,96},{80,112},{96,64},{112,80},{1... | collective-permute-start | bytes 1081352 | tf_op jit(solution)/shard_map/ppermute | solution.py:13
  709.6 20.1 %collective-permute-start.15 = (bf16[128,1408]{1,0:T(8,128)(2,1)S(1)}, bf16[128,1408]{1,0:T(8,128)(2,1)}, u32[]{:S(2)}, u32[]{:S(2)}) collective-permute-start(bf16[128,1408]{1,0:T(8,128)(2,1)S(1)} %collective-permute-done.14), channel_id=1, source_target_pairs={{0,64},{16,80},{32,96},{48,112},{64,0},{80,16},{96,32},{112,48},{1... | collective-permute-start | bytes 1081352 | tf_op jit(solution)/shard_map/ppermute | solution.py:13
  729.7 38.5 %collective-permute-start.16 = (bf16[128,1408]{1,0:T(8,128)(2,1)}, bf16[128,1408]{1,0:T(8,128)(2,1)}, u32[]{:S(2)}, u32[]{:S(2)}) collective-permute-start(bf16[128,1408]{1,0:T(8,128)(2,1)} %collective-permute-done.15), channel_id=1, source_target_pairs={{0,128},{16,144},{32,160},{48,176},{64,192},{80,208},{96,224},{112... | collective-permute-start | bytes 1081352 | tf_op jit(solution)/shard_map/ppermute | solution.py:13
  738.6 50.7 %collective-permute-start.12 = (bf16[128,1408]{1,0:T(8,128)(2,1)}, bf16[128,1408]{1,0:T(8,128)(2,1)}, u32[]{:S(2)}, u32[]{:S(2)}) collective-permute-start(bf16[128,1408]{1,0:T(8,128)(2,1)} %bitcast.139), channel_id=1, source_target_pairs={{16,0},{32,16},{48,32},{64,48},{80,64},{96,80},{112,96},{128,112},... | collective-permute-start | bytes 1081352 | tf_op jit(solution)/shard_map/ppermute | solution.py:19
  768.2 33.0 %collective-permute-start.17 = (bf16[128,1408]{1,0:T(8,128)(2,1)}, bf16[128,1408]{1,0:T(8,128)(2,1)}, u32[]{:S(2)}, u32[]{:S(2)}) collective-permute-start(bf16[128,1408]{1,0:T(8,128)(2,1)} %collective-permute-done.16), channel_id=1, source_target_pairs={{0,256},{16,272},{32,288},{48,304},{64,320},{80,336},{96,352},{112... | collective-permute-start | bytes 1081352 | tf_op jit(solution)/shard_map/ppermute | solution.py:13
  787.8 1.2 copy-start.22
  787.8 1.2 copy-start.2
  789.2 14.0 %copy-start.25 = (f32[128,384]{1,0:T(8,128)S(1)}, f32[128,384]{1,0:T(8,128)}, u32[]{:S(2)}) copy-start(f32[128,384]{1,0:T(8,128)} %get-tuple-element.34) | copy-start | bytes 589828
  789.3 14.0 %copy-start.40 = (bf16[1,384,1408]{2,1,0:T(8,128)(2,1)S(1)}, bf16[1,384,1408]{2,1,0:T(8,128)(2,1)}, u32[]{:S(2)}) copy-start(bf16[1,384,1408]{2,1,0:T(8,128)(2,1)} %all-gather.4.cloned.1.call-done) | copy-start | bytes 3244036
  802.5 0.7 copy-start.18
  804.4 1.4 copy-start.7
  804.4 1.4 copy-start.12
  805.7 125.8 %reduce-scatter.12.cloned.1.call-start = ((), (), s32[]{:S(2)}) async-start(), calls=%async_computation.12 | async-start | bytes 1622016
  815.5 0.9 copy-start.35
  815.5 149.6 %reduce-scatter.10.cloned.1.call-start = ((), (), s32[]{:S(2)}) async-start(), calls=%async_computation.11 | async-start | bytes 1486848
  818.3 73.6 %copy-start.19 = (bf16[128,1408]{1,0:T(8,128)(2,1)S(1)}, bf16[128,1408]{1,0:T(8,128)(2,1)}, u32[]{:S(2)}) copy-start(bf16[128,1408]{1,0:T(8,128)(2,1)} %copy-done.18) | copy-start | bytes 1081348
  821.3 72.6 %copy-start.5 = (bf16[128,1408]{1,0:T(8,128)(2,1)S(1)}, bf16[128,1408]{1,0:T(8,128)(2,1)}, u32[]{:S(2)}) copy-start(bf16[128,1408]{1,0:T(8,128)(2,1)} %copy-done.4) | copy-start | bytes 1081348
  821.3 72.6 %copy-start.11 = (bf16[128,1408]{1,0:T(8,128)(2,1)S(1)}, bf16[128,1408]{1,0:T(8,128)(2,1)}, u32[]{:S(2)}) copy-start(bf16[128,1408]{1,0:T(8,128)(2,1)} %copy-done.10) | copy-start | bytes 1081348
  821.3 72.6 %copy-start.16 = (bf16[128,1408]{1,0:T(8,128)(2,1)S(1)}, bf16[128,1408]{1,0:T(8,128)(2,1)}, u32[]{:S(2)}) copy-start(bf16[128,1408]{1,0:T(8,128)(2,1)} %copy-done.15) | copy-start | bytes 1081348
  891.9 2.0 copy-start.31
  891.9 2.0 copy-start.32
  891.9 2.0 copy-start.33
  891.9 2.0 copy-start.34
  895.4 1.1 copy-start.9
  895.4 1.3 copy-start.14
  896.5 103.8 %reduce-scatter.8.cloned.1.call-start = ((), (), s32[]{:S(2)}) async-start(), calls=%async_computation.10 | async-start | bytes 1622016 | tf_op jit(solution)/shard_map/reduce_scatter | solution.py:120
  899.7 1.0 copy-start.21
  (5 other events, 3.4 us)
Sparse Core Ops, SparseCore 0:
  10.1 39.1 all-gather.5
  51.4 33.3 all-gather.3
  88.6 85.4 all-reduce.4
  176.0 49.4 all-gather.7
  328.0 87.0 all-reduce.6
  566.7 86.1 all-reduce.8
  805.8 86.0 all-reduce.10
  894.7 36.7 reduce-scatter.11
  934.2 30.8 reduce-scatter.9
  968.4 31.8 reduce-scatter.7
where the time goes:
time: 1010 us
  waiting for transfers between devices  646 us (64%)
  starting transfers between devices  153 us (15%)
  blocking collectives  108 us (11%)
  local copies, waits for them, and re-layouts  51.2 us (5%)
  matrix products  23.4 us (2%)
  between operations  14.9 us (1%)
  other arithmetic  10.5 us (1%)
    psum x4, waiting for transfers between devices, body(): back_mixed = upstream.astype(jnp.float32) + lax.psum(partial_back, 'tensor')  312 us
    ppermute x15, waiting for transfers between devices, from_partner(): return lax.ppermute(value, axis, pairs)  188 us
    ppermute x15, starting transfers between devices, from_partner(): return lax.ppermute(value, axis, pairs)  141 us
    all_gather x3, blocking collectives, body(): payload = lax.all_gather(input_grad, 'tensor', axis=2, tiled=True)  70.2 us
    unnamed x12, waiting for transfers between devices  63 us
    unnamed x100, local copies, waits for them, and re-layouts  34.3 us
    reduce_scatter x1, waiting for transfers between devices, body(): lax.psum_scatter(down_total[None].astype(jnp.bfloat16), 'replica', scatte...  33.1 us
    all_gather x1, waiting for transfers between devices, body(): lax.all_gather(w_down, 'replica', axis=1, tiled=True)  33.1 us
  transfers between devices with their start and end apart: 28, of which 24 were waited for; matrix products, arithmetic and copies ran while one was open for 5% of the time, Pallas kernels for 0%

commit v1 on v0

--- a/solution.py
+++ b/solution.py
@@ -90,7 +90,8 @@
         kept_grads.append(mixed_grad)
         kept_upstream.append(upstream)
         if tick_index + 1 < tick_count:
-            payload = lax.all_gather(input_grad, "tensor", axis=2, tiled=True)
+            outgoing = jnp.stack([input_grad] * lax.axis_size("tensor"))
+            payload = jnp.concatenate(lax.all_to_all(outgoing, "tensor", 0, 0), axis=2)
             from_above = shifted(payload[:, 0], "section", -1)
             mirrored = reflect(payload[:, 1], section_count)
             summed = (

time: 1010 us -> 953 us (0.944)
  blocking collectives: 108 us -> 59 us
  starting transfers between devices: 153 us -> 141 us
    all_gather x3 -> x0, blocking collectives: 70.2 us -> none  [body(): payload = lax.all_gather(input_grad, 'tensor', axis=2, tiled=True)]
    all_to_all x0 -> x2, blocking collectives: none -> 21.5 us  [body(): payload = jnp.concatenate(lax.all_to_all(outgoing, 'tensor', 0, 0), axis=2)]
    ppermute x15, starting transfers between devices: 141 us -> 126 us  [from_partner(): return lax.ppermute(value, axis, pairs)]
    unnamed x100 -> x96, local copies, waits for them, and re-layouts: 34.3 us -> 34.5 us
  transfers between devices with their start and end apart: 28 -> 29, of which waited for: 24 -> 25; matrix products, arithmetic and copies ran while one was open for 5% -> 5% of each run, Pallas kernels for 0% -> 0%
where the time goes in v1:
time: 953 us; the launch traced here: 951 us
  waiting for transfers between devices  655 us (69%)
  starting transfers between devices  141 us (15%)
  blocking collectives  59 us (6%)
  local copies, waits for them, and re-layouts  48.2 us (5%)
  matrix products  23.4 us (2%)
  between operations  14.9 us (2%)
  other arithmetic  9.75 us (1%)
    psum x4, waiting for transfers between devices, body(): back_mixed = upstream.astype(jnp.float32) + lax.psum(partial_back, 'tensor')  315 us
    ppermute x15, waiting for transfers between devices, from_partner(): return lax.ppermute(value, axis, pairs)  187 us
    ppermute x15, starting transfers between devices, from_partner(): return lax.ppermute(value, axis, pairs)  126 us
    unnamed x12, waiting for transfers between devices  63 us
    unnamed x96, local copies, waits for them, and re-layouts  34.5 us
    reduce_scatter x1, waiting for transfers between devices, body(): lax.psum_scatter(down_total[None].astype(jnp.bfloat16), 'replica', scatte...  33.1 us
    all_gather x1, waiting for transfers between devices, body(): lax.all_gather(w_down, 'replica', axis=1, tiled=True)  33.1 us
    all_gather x1, blocking collectives, body(): lax.all_gather(incoming, 'tensor', axis=2, tiled=True)  23.1 us
  transfers between devices with their start and end apart: 29, of which 25 were waited for; matrix products, arithmetic and copies ran while one was open for 5% of the time, Pallas kernels for 0%

profile of v1, /device:TPU:1, one launch (start us, length us, event | category | flops | bytes accessed | tf_op | source)
XLA Modules:
  0.0 951.2 jit_solution(9283304016955087848)
XLA Ops:
  9.7 23.1 %all_gather.15 = bf16[1,128,1408]{1,2,0:T(8,128)(2,1)S(1)} all-gather(bf16[1,128,176]{1,2,0:T(8,128)(2,1)S(1)} %copy-done.34), channel_id=1, replica_groups=mesh['section'=32,'tensor'=8,'replica'=2] {'tensor'}, dimensions={2}, use_global_device_ids=true | all-gather | bytes 405504 | tf_op jit(solution)/shard_map/all_gather | solution.py:50
  32.8 16.5 %all-gather.6.cloned.1.call-done = bf16[1,1408,384]{1,2,0:T(8,128)(2,1)} async-done(((bf16[1,1408,192]{1,2,0:T(8,128)(2,1)}), bf16[1,1408,384]{1,2,0:T(8,128)(2,1)}) %all-gather.6.cloned.1.call-update) | async-done | bytes 1081360 | tf_op jit(solution)/shard_map/all_gather | solution.py:43
  49.3 2.4 multiply_convert_fusion.3
  51.7 33.1 %all-gather.4.cloned.1.call-done = bf16[1,384,1408]{2,1,0:T(8,128)(2,1)} async-done(((bf16[1,192,1408]{2,1,0:T(8,128)(2,1)}), bf16[1,384,1408]{2,1,0:T(8,128)(2,1)}) %all-gather.4.cloned.1.call-update) | async-done | bytes 1081360 | tf_op jit(solution)/shard_map/all_gather | solution.py:44
  84.8 1.7 fusion.23
  88.9 14.3 %all_gather.19 = bf16[1,2,176,1408]{3,2,1,0:T(8,128)(2,1)S(1)} all-gather(bf16[1,2,88,1408]{3,2,1,0:T(8,128)(2,1)S(1)} %copy-done.21), channel_id=1, replica_groups=mesh['section'=32,'tensor'=8,'replica'=2] {'replica'}, dimensions={2}, use_global_device_ids=true | all-gather | bytes 1486848 | tf_op jit(solution)/shard_map/all_gather | solution.py:42
  103.2 70.2 %all-reduce.5.cloned.1.call-done = f32[128,1408]{1,0:T(8,128)} async-done(((f32[128,1408]{1,0:T(8,128)}), f32[128,1408]{1,0:T(8,128)}) %all-reduce.5.cloned.1.call-update) | async-done | bytes 720912 | tf_op jit(solution)/shard_map/psum | solution.py:81
  176.8 3.5 all-to-all-start
  181.0 7.3 all-to-all-done
  189.3 8.7 collective-permute-start.1
  198.0 1.5 collective-permute-done.1
  199.5 3.1 collective-permute-start.2
  202.7 8.5 collective-permute-done.2
  211.1 4.1 collective-permute-start.3
  215.3 15.8 %collective-permute-done.3 = bf16[128,1408]{1,0:T(8,128)(2,1)} collective-permute-done((bf16[128,1408]{1,0:T(8,128)(2,1)S(1)}, bf16[128,1408]{1,0:T(8,128)(2,1)}, u32[]{:S(2)}, u32[]{:S(2)}) %collective-permute-start.3) | collective-permute-done | bytes 360480 | tf_op jit(solution)/shard_map/ppermute | solution.py:13
  231.0 7.3 collective-permute-start.4
  241.4 3.7 collective-permute-start
  245.1 24.5 %collective-permute-done.4 = bf16[128,1408]{1,0:T(8,128)(2,1)} collective-permute-done((bf16[128,1408]{1,0:T(8,128)(2,1)}, bf16[128,1408]{1,0:T(8,128)(2,1)}, u32[]{:S(2)}, u32[]{:S(2)}) %collective-permute-start.4) | collective-permute-done | bytes 360480 | tf_op jit(solution)/shard_map/ppermute | solution.py:13
  269.6 18.9 %collective-permute-start.5 = (bf16[128,1408]{1,0:T(8,128)(2,1)}, bf16[128,1408]{1,0:T(8,128)(2,1)}, u32[]{:S(2)}, u32[]{:S(2)}) collective-permute-start(bf16[128,1408]{1,0:T(8,128)(2,1)} %collective-permute-done.4), channel_id=1, source_target_pairs={{0,256},{16,272},{32,288},{48,304},{64,320},{80,336},{96,352},{112... | collective-permute-start | bytes 1081352 | tf_op jit(solution)/shard_map/ppermute | solution.py:13
  288.6 2.0 fusion.108
  290.6 1.9 copy.57
  292.5 10.6 %collective-permute-done.5 = bf16[128,1408]{1,0:T(8,128)(2,1)} collective-permute-done((bf16[128,1408]{1,0:T(8,128)(2,1)}, bf16[128,1408]{1,0:T(8,128)(2,1)}, u32[]{:S(2)}, u32[]{:S(2)}) %collective-permute-start.5) | collective-permute-done | bytes 360480 | tf_op jit(solution)/shard_map/ppermute | solution.py:13
  303.0 1.4 fusion.66
  307.6 86.6 %all-reduce.7.cloned.1.call-done = f32[128,1408]{1,0:T(8,128)} async-done(((f32[128,1408]{1,0:T(8,128)}), f32[128,1408]{1,0:T(8,128)}) %all-reduce.7.cloned.1.call-update) | async-done | bytes 720912 | tf_op jit(solution)/shard_map/psum | solution.py:81
  396.8 10.8 %all_to_all.15 = bf16[8,128,2,176]{1,3,2,0:T(8,128)(2,1)S(1)} all-to-all(bf16[8,128,2,176]{1,3,2,0:T(8,128)(2,1)S(1)} %stack.13), channel_id=1, replica_groups=mesh['section'=32,'tensor'=8,'replica'=2] {'tensor'}, dimensions={0} | all-to-all | bytes 1441792 | tf_op jit(solution)/shard_map/all_to_all | solution.py:94
  408.5 1.9 copy.62
  410.4 8.9 collective-permute-start.7
  419.3 1.5 collective-permute-done.7
  420.8 3.0 collective-permute-start.8
  423.9 8.5 collective-permute-done.8
  432.3 4.0 collective-permute-start.9
  436.4 16.0 %collective-permute-done.9 = bf16[128,1408]{1,0:T(8,128)(2,1)} collective-permute-done((bf16[128,1408]{1,0:T(8,128)(2,1)S(1)}, bf16[128,1408]{1,0:T(8,128)(2,1)}, u32[]{:S(2)}, u32[]{:S(2)}) %collective-permute-start.9) | collective-permute-done | bytes 360480 | tf_op jit(solution)/shard_map/ppermute | solution.py:13
  452.4 7.1 collective-permute-start.10
  459.4 1.9 copy.61
  461.3 3.7 collective-permute-start.6
  465.1 25.8 %collective-permute-done.10 = bf16[128,1408]{1,0:T(8,128)(2,1)} collective-permute-done((bf16[128,1408]{1,0:T(8,128)(2,1)}, bf16[128,1408]{1,0:T(8,128)(2,1)}, u32[]{:S(2)}, u32[]{:S(2)}) %collective-permute-start.10) | collective-permute-done | bytes 360480 | tf_op jit(solution)/shard_map/ppermute | solution.py:13
  490.9 18.7 %collective-permute-start.11 = (bf16[128,1408]{1,0:T(8,128)(2,1)}, bf16[128,1408]{1,0:T(8,128)(2,1)}, u32[]{:S(2)}, u32[]{:S(2)}) collective-permute-start(bf16[128,1408]{1,0:T(8,128)(2,1)} %collective-permute-done.10), channel_id=1, source_target_pairs={{0,256},{16,272},{32,288},{48,304},{64,320},{80,336},{96,352},{112... | collective-permute-start | bytes 1081352 | tf_op jit(solution)/shard_map/ppermute | solution.py:13
  509.6 1.6 gather_fusion.6
  511.3 2.2 multiply_convert_fusion.1
  514.4 9.6 %collective-permute-done.11 = bf16[128,1408]{1,0:T(8,128)(2,1)} collective-permute-done((bf16[128,1408]{1,0:T(8,128)(2,1)}, bf16[128,1408]{1,0:T(8,128)(2,1)}, u32[]{:S(2)}, u32[]{:S(2)}) %collective-permute-start.11) | collective-permute-done | bytes 360480 | tf_op jit(solution)/shard_map/ppermute | solution.py:13
  524.0 1.4 fusion.67
  527.8 87.0 %all-reduce.9.cloned.1.call-done = f32[128,1408]{1,0:T(8,128)} async-done(((f32[128,1408]{1,0:T(8,128)}), f32[128,1408]{1,0:T(8,128)}) %all-reduce.9.cloned.1.call-update) | async-done | bytes 720912 | tf_op jit(solution)/shard_map/psum | solution.py:81
  617.3 10.8 %all_to_all.16 = bf16[8,128,2,176]{1,3,2,0:T(8,128)(2,1)S(1)} all-to-all(bf16[8,128,2,176]{1,3,2,0:T(8,128)(2,1)S(1)} %stack.14), channel_id=1, replica_groups=mesh['section'=32,'tensor'=8,'replica'=2] {'tensor'}, dimensions={0} | all-to-all | bytes 1441792 | tf_op jit(solution)/shard_map/all_to_all | solution.py:94
  629.0 1.9 copy.65
  630.8 8.9 collective-permute-start.13
  639.8 1.5 collective-permute-done.13
  641.3 3.0 collective-permute-start.14
  644.3 8.5 collective-permute-done.14
  652.8 4.0 collective-permute-start.15
  656.8 16.0 %collective-permute-done.15 = bf16[128,1408]{1,0:T(8,128)(2,1)} collective-permute-done((bf16[128,1408]{1,0:T(8,128)(2,1)S(1)}, bf16[128,1408]{1,0:T(8,128)(2,1)}, u32[]{:S(2)}, u32[]{:S(2)}) %collective-permute-start.15) | collective-permute-done | bytes 360480 | tf_op jit(solution)/shard_map/ppermute | solution.py:13
  672.8 7.1 collective-permute-start.16
  680.8 3.7 collective-permute-start.12
  684.5 26.8 %collective-permute-done.16 = bf16[128,1408]{1,0:T(8,128)(2,1)} collective-permute-done((bf16[128,1408]{1,0:T(8,128)(2,1)}, bf16[128,1408]{1,0:T(8,128)(2,1)}, u32[]{:S(2)}, u32[]{:S(2)}) %collective-permute-start.16) | collective-permute-done | bytes 360480 | tf_op jit(solution)/shard_map/ppermute | solution.py:13
  711.3 18.9 %collective-permute-start.17 = (bf16[128,1408]{1,0:T(8,128)(2,1)}, bf16[128,1408]{1,0:T(8,128)(2,1)}, u32[]{:S(2)}, u32[]{:S(2)}) collective-permute-start(bf16[128,1408]{1,0:T(8,128)(2,1)} %collective-permute-done.16), channel_id=1, source_target_pairs={{0,256},{16,272},{32,288},{48,304},{64,320},{80,336},{96,352},{112... | collective-permute-start | bytes 1081352 | tf_op jit(solution)/shard_map/ppermute | solution.py:13
  732.6 11.8 %collective-permute-done.17 = bf16[128,1408]{1,0:T(8,128)(2,1)} collective-permute-done((bf16[128,1408]{1,0:T(8,128)(2,1)}, bf16[128,1408]{1,0:T(8,128)(2,1)}, u32[]{:S(2)}, u32[]{:S(2)}) %collective-permute-start.17) | collective-permute-done | bytes 360480 | tf_op jit(solution)/shard_map/ppermute | solution.py:13
  749.0 2.2 fusion
  751.1 4.8 copy.53
  756.0 2.7 copy.68
  764.7 71.2 %all-reduce.11.cloned.1.call-done = f32[128,1408]{1,0:T(8,128)} async-done(((f32[128,1408]{1,0:T(8,128)}), f32[128,1408]{1,0:T(8,128)}) %all-reduce.11.cloned.1.call-update) | async-done | bytes 720912 | tf_op jit(solution)/shard_map/psum | solution.py:81
  840.7 3.0 fusion.1
  845.8 29.7 %reduce-scatter.12.cloned.1.call-done = bf16[192,1408]{1,0:T(8,128)(2,1)} async-done(((bf16[384,1408]{1,0:T(8,128)(2,1)}), bf16[192,1408]{1,0:T(8,128)(2,1)}) %reduce-scatter.12.cloned.1.call-update) | async-done | bytes 540688
  875.5 1.6 reshape_bitcast_fusion
  878.0 31.3 %reduce-scatter.10.cloned.1.call-done = bf16[88,2816]{1,0:T(8,128)(2,1)} async-done(((bf16[176,2816]{1,0:T(8,128)(2,1)}), bf16[88,2816]{1,0:T(8,128)(2,1)}) %reduce-scatter.10.cloned.1.call-update) | async-done | bytes 495632
  911.2 33.1 %reduce-scatter.8.cloned.1.call-done = bf16[1,192,1408]{2,1,0:T(8,128)(2,1)} async-done(((bf16[1,384,1408]{2,1,0:T(8,128)(2,1)}), bf16[1,192,1408]{2,1,0:T(8,128)(2,1)}) %reduce-scatter.8.cloned.1.call-update) | async-done | bytes 540688 | tf_op jit(solution)/shard_map/reduce_scatter | solution.py:121
  (160 shorter events, 49.3 us)
Async XLA Ops:
  7.2 1.6 copy-start
  7.2 1.5 copy-start.35
  7.2 42.2 %all-gather.6.cloned.1.call-start = ((), (), s32[]{:S(2)}) async-start(), calls=%async_computation.7 | async-start | bytes 1622016 | tf_op jit(solution)/shard_map/all_gather | solution.py:43
  7.9 76.9 %all-gather.4.cloned.1.call-start = ((), (), s32[]{:S(2)}) async-start(), calls=%async_computation.6 | async-start | bytes 1622016 | tf_op jit(solution)/shard_map/all_gather | solution.py:44
  8.7 164.8 %all-reduce.5.cloned.1.call-start = ((), (), s32[]{:S(2)}) async-start(), calls=%async_computation.8 | async-start | bytes 1441792 | tf_op jit(solution)/shard_map/psum | solution.py:81
  8.8 0.9 copy-start.34
  9.7 76.9 %copy-start.4 = (bf16[128,1408]{1,0:T(8,128)(2,1)}, bf16[128,1408]{1,0:T(8,128)(2,1)S(1)}, u32[]{:S(2)}) copy-start(bf16[128,1408]{1,0:T(8,128)(2,1)S(1)} %gather_fusion.4) | copy-start | bytes 1081348
  51.7 34.9 %copy-start.1 = (bf16[1,1408,384]{1,2,0:T(8,128)(2,1)S(1)}, bf16[1,1408,384]{1,2,0:T(8,128)(2,1)}, u32[]{:S(2)}) copy-start(bf16[1,1408,384]{1,2,0:T(8,128)(2,1)} %all-gather.6.cloned.1.call-done) | copy-start | bytes 3244036
  86.6 1.3 copy-start.25
  87.8 1.0 copy-start.21
  174.7 0.7 copy-start.2
  176.8 11.5 %all-to-all-start = ((bf16[8,128,2,176]{1,3,2,0:T(8,128)(2,1)}), bf16[8,128,2,176]{1,3,2,0:T(8,128)(2,1)S(1)}, u32[]{:S(2)}, u32[]{:S(2)}) async-start(bf16[8,128,2,176]{1,3,2,0:T(8,128)(2,1)} %stack.12), calls=%async_computation | async-start | bytes 1441792 | tf_op jit(solution)/shard_map/all_to_all | solution.py:94
  180.4 108.2 %all-gather.8.cloned.1.call-start = ((), (), s32[]{:S(2)}) async-start(), calls=%async_computation.9 | async-start | bytes 1216512 | tf_op jit(solution)/shard_map/all_gather | solution.py:51
  180.9 213.3 %all-reduce.7.cloned.1.call-start = ((), (), s32[]{:S(2)}) async-start(), calls=%async_computation.10 | async-start | bytes 1441792 | tf_op jit(solution)/shard_map/psum | solution.py:81
  189.3 10.2 %collective-permute-start.1 = (bf16[128,1408]{1,0:T(8,128)(2,1)}, bf16[128,1408]{1,0:T(8,128)(2,1)S(1)}, u32[]{:S(2)}, u32[]{:S(2)}) collective-permute-start(bf16[128,1408]{1,0:T(8,128)(2,1)} %bitcast.153), channel_id=1, source_target_pairs={{0,16},{16,0},{32,48},{48,32},{64,80},{80,64},{96,112},{112,96},{1... | collective-permute-start | bytes 1081352 | tf_op jit(solution)/shard_map/ppermute | solution.py:13
  199.5 11.6 %collective-permute-start.2 = (bf16[128,1408]{1,0:T(8,128)(2,1)S(1)}, bf16[128,1408]{1,0:T(8,128)(2,1)S(1)}, u32[]{:S(2)}, u32[]{:S(2)}) collective-permute-start(bf16[128,1408]{1,0:T(8,128)(2,1)S(1)} %collective-permute-done.1), channel_id=1, source_target_pairs={{0,32},{16,48},{32,0},{48,16},{64,96},{80,112},{96,64},{112,80},{1... | collective-permute-start | bytes 1081352 | tf_op jit(solution)/shard_map/ppermute | solution.py:13
  211.1 19.9 %collective-permute-start.3 = (bf16[128,1408]{1,0:T(8,128)(2,1)S(1)}, bf16[128,1408]{1,0:T(8,128)(2,1)}, u32[]{:S(2)}, u32[]{:S(2)}) collective-permute-start(bf16[128,1408]{1,0:T(8,128)(2,1)S(1)} %collective-permute-done.2), channel_id=1, source_target_pairs={{0,64},{16,80},{32,96},{48,112},{64,0},{80,16},{96,32},{112,48},{1... | collective-permute-start | bytes 1081352 | tf_op jit(solution)/shard_map/ppermute | solution.py:13
  231.0 38.6 %collective-permute-start.4 = (bf16[128,1408]{1,0:T(8,128)(2,1)}, bf16[128,1408]{1,0:T(8,128)(2,1)}, u32[]{:S(2)}, u32[]{:S(2)}) collective-permute-start(bf16[128,1408]{1,0:T(8,128)(2,1)} %collective-permute-done.3), channel_id=1, source_target_pairs={{0,128},{16,144},{32,160},{48,176},{64,192},{80,208},{96,224},{112... | collective-permute-start | bytes 1081352 | tf_op jit(solution)/shard_map/ppermute | solution.py:13
  239.3 2.1 copy-start.10
  241.4 51.1 %collective-permute-start = (bf16[128,1408]{1,0:T(8,128)(2,1)}, bf16[128,1408]{1,0:T(8,128)(2,1)}, u32[]{:S(2)}, u32[]{:S(2)}) collective-permute-start(bf16[128,1408]{1,0:T(8,128)(2,1)} %bitcast.150), channel_id=1, source_target_pairs={{16,0},{32,16},{48,32},{64,48},{80,64},{96,80},{112,96},{128,112},... | collective-permute-start | bytes 1081352 | tf_op jit(solution)/shard_map/ppermute | solution.py:19
  269.6 33.4 %collective-permute-start.5 = (bf16[128,1408]{1,0:T(8,128)(2,1)}, bf16[128,1408]{1,0:T(8,128)(2,1)}, u32[]{:S(2)}, u32[]{:S(2)}) collective-permute-start(bf16[128,1408]{1,0:T(8,128)(2,1)} %collective-permute-done.4), channel_id=1, source_target_pairs={{0,256},{16,272},{32,288},{48,304},{64,320},{80,336},{96,352},{112... | collective-permute-start | bytes 1081352 | tf_op jit(solution)/shard_map/ppermute | solution.py:13
  292.5 12.7 %copy-start.22 = (f32[128,384]{1,0:T(8,128)S(1)}, f32[128,384]{1,0:T(8,128)}, u32[]{:S(2)}) copy-start(f32[128,384]{1,0:T(8,128)} %get-tuple-element.38) | copy-start | bytes 589828
  292.5 12.7 %copy-start.36 = (bf16[1,384,1408]{2,1,0:T(8,128)(2,1)S(1)}, bf16[1,384,1408]{2,1,0:T(8,128)(2,1)}, u32[]{:S(2)}) copy-start(bf16[1,384,1408]{2,1,0:T(8,128)(2,1)} %all-gather.4.cloned.1.call-done) | copy-start | bytes 3244036
  304.4 0.7 copy-start.6
  307.6 307.3 %all-reduce.9.cloned.1.call-start = ((), (), s32[]{:S(2)}) async-start(), calls=%async_computation.11 | async-start | bytes 1441792 | tf_op jit(solution)/shard_map/psum | solution.py:81
  395.5 0.7 copy-start.8
  410.4 10.4 %collective-permute-start.7 = (bf16[128,1408]{1,0:T(8,128)(2,1)}, bf16[128,1408]{1,0:T(8,128)(2,1)S(1)}, u32[]{:S(2)}, u32[]{:S(2)}) collective-permute-start(bf16[128,1408]{1,0:T(8,128)(2,1)} %bitcast.154), channel_id=1, source_target_pairs={{0,16},{16,0},{32,48},{48,32},{64,80},{80,64},{96,112},{112,96},{1... | collective-permute-start | bytes 1081352 | tf_op jit(solution)/shard_map/ppermute | solution.py:13
  420.8 11.5 %collective-permute-start.8 = (bf16[128,1408]{1,0:T(8,128)(2,1)S(1)}, bf16[128,1408]{1,0:T(8,128)(2,1)S(1)}, u32[]{:S(2)}, u32[]{:S(2)}) collective-permute-start(bf16[128,1408]{1,0:T(8,128)(2,1)S(1)} %collective-permute-done.7), channel_id=1, source_target_pairs={{0,32},{16,48},{32,0},{48,16},{64,96},{80,112},{96,64},{112,80},{1... | collective-permute-start | bytes 1081352 | tf_op jit(solution)/shard_map/ppermute | solution.py:13
  432.3 20.0 %collective-permute-start.9 = (bf16[128,1408]{1,0:T(8,128)(2,1)S(1)}, bf16[128,1408]{1,0:T(8,128)(2,1)}, u32[]{:S(2)}, u32[]{:S(2)}) collective-permute-start(bf16[128,1408]{1,0:T(8,128)(2,1)S(1)} %collective-permute-done.8), channel_id=1, source_target_pairs={{0,64},{16,80},{32,96},{48,112},{64,0},{80,16},{96,32},{112,48},{1... | collective-permute-start | bytes 1081352 | tf_op jit(solution)/shard_map/ppermute | solution.py:13
  452.4 38.5 %collective-permute-start.10 = (bf16[128,1408]{1,0:T(8,128)(2,1)}, bf16[128,1408]{1,0:T(8,128)(2,1)}, u32[]{:S(2)}, u32[]{:S(2)}) collective-permute-start(bf16[128,1408]{1,0:T(8,128)(2,1)} %collective-permute-done.9), channel_id=1, source_target_pairs={{0,128},{16,144},{32,160},{48,176},{64,192},{80,208},{96,224},{112... | collective-permute-start | bytes 1081352 | tf_op jit(solution)/shard_map/ppermute | solution.py:13
  461.3 53.0 %collective-permute-start.6 = (bf16[128,1408]{1,0:T(8,128)(2,1)}, bf16[128,1408]{1,0:T(8,128)(2,1)}, u32[]{:S(2)}, u32[]{:S(2)}) collective-permute-start(bf16[128,1408]{1,0:T(8,128)(2,1)} %bitcast.152), channel_id=1, source_target_pairs={{16,0},{32,16},{48,32},{64,48},{80,64},{96,80},{112,96},{128,112},... | collective-permute-start | bytes 1081352 | tf_op jit(solution)/shard_map/ppermute | solution.py:19
  490.9 33.1 %collective-permute-start.11 = (bf16[128,1408]{1,0:T(8,128)(2,1)}, bf16[128,1408]{1,0:T(8,128)(2,1)}, u32[]{:S(2)}, u32[]{:S(2)}) collective-permute-start(bf16[128,1408]{1,0:T(8,128)(2,1)} %collective-permute-done.10), channel_id=1, source_target_pairs={{0,256},{16,272},{32,288},{48,304},{64,320},{80,336},{96,352},{112... | collective-permute-start | bytes 1081352 | tf_op jit(solution)/shard_map/ppermute | solution.py:13
  514.4 11.0 %copy-start.24 = (f32[128,384]{1,0:T(8,128)S(1)}, f32[128,384]{1,0:T(8,128)}, u32[]{:S(2)}) copy-start(f32[128,384]{1,0:T(8,128)} %get-tuple-element.36) | copy-start | bytes 589828
  514.4 11.0 %copy-start.37 = (bf16[1,384,1408]{2,1,0:T(8,128)(2,1)S(1)}, bf16[1,384,1408]{2,1,0:T(8,128)(2,1)}, u32[]{:S(2)}) copy-start(bf16[1,384,1408]{2,1,0:T(8,128)(2,1)} %all-gather.4.cloned.1.call-done) | copy-start | bytes 3244036
  525.4 89.5 %copy-start.12 = (bf16[128,1408]{1,0:T(8,128)(2,1)}, bf16[128,1408]{1,0:T(8,128)(2,1)S(1)}, u32[]{:S(2)}) copy-start(bf16[128,1408]{1,0:T(8,128)(2,1)S(1)} %fusion.67) | copy-start | bytes 1081348
  527.8 308.1 %all-reduce.11.cloned.1.call-start = ((), (), s32[]{:S(2)}) async-start(), calls=%async_computation.12 | async-start | bytes 1441792 | tf_op jit(solution)/shard_map/psum | solution.py:81
  630.8 10.4 %collective-permute-start.13 = (bf16[128,1408]{1,0:T(8,128)(2,1)}, bf16[128,1408]{1,0:T(8,128)(2,1)S(1)}, u32[]{:S(2)}, u32[]{:S(2)}) collective-permute-start(bf16[128,1408]{1,0:T(8,128)(2,1)} %bitcast.155), channel_id=1, source_target_pairs={{0,16},{16,0},{32,48},{48,32},{64,80},{80,64},{96,112},{112,96},{1... | collective-permute-start | bytes 1081352 | tf_op jit(solution)/shard_map/ppermute | solution.py:13
  641.3 11.5 %collective-permute-start.14 = (bf16[128,1408]{1,0:T(8,128)(2,1)S(1)}, bf16[128,1408]{1,0:T(8,128)(2,1)S(1)}, u32[]{:S(2)}, u32[]{:S(2)}) collective-permute-start(bf16[128,1408]{1,0:T(8,128)(2,1)S(1)} %collective-permute-done.13), channel_id=1, source_target_pairs={{0,32},{16,48},{32,0},{48,16},{64,96},{80,112},{96,64},{112,80},{1... | collective-permute-start | bytes 1081352 | tf_op jit(solution)/shard_map/ppermute | solution.py:13
  652.8 20.0 %collective-permute-start.15 = (bf16[128,1408]{1,0:T(8,128)(2,1)S(1)}, bf16[128,1408]{1,0:T(8,128)(2,1)}, u32[]{:S(2)}, u32[]{:S(2)}) collective-permute-start(bf16[128,1408]{1,0:T(8,128)(2,1)S(1)} %collective-permute-done.14), channel_id=1, source_target_pairs={{0,64},{16,80},{32,96},{48,112},{64,0},{80,16},{96,32},{112,48},{1... | collective-permute-start | bytes 1081352 | tf_op jit(solution)/shard_map/ppermute | solution.py:13
  672.8 38.5 %collective-permute-start.16 = (bf16[128,1408]{1,0:T(8,128)(2,1)}, bf16[128,1408]{1,0:T(8,128)(2,1)}, u32[]{:S(2)}, u32[]{:S(2)}) collective-permute-start(bf16[128,1408]{1,0:T(8,128)(2,1)} %collective-permute-done.15), channel_id=1, source_target_pairs={{0,128},{16,144},{32,160},{48,176},{64,192},{80,208},{96,224},{112... | collective-permute-start | bytes 1081352 | tf_op jit(solution)/shard_map/ppermute | solution.py:13
  680.8 51.8 %collective-permute-start.12 = (bf16[128,1408]{1,0:T(8,128)(2,1)}, bf16[128,1408]{1,0:T(8,128)(2,1)}, u32[]{:S(2)}, u32[]{:S(2)}) collective-permute-start(bf16[128,1408]{1,0:T(8,128)(2,1)} %bitcast.151), channel_id=1, source_target_pairs={{16,0},{32,16},{48,32},{64,48},{80,64},{96,80},{112,96},{128,112},... | collective-permute-start | bytes 1081352 | tf_op jit(solution)/shard_map/ppermute | solution.py:19
  711.3 33.2 %collective-permute-start.17 = (bf16[128,1408]{1,0:T(8,128)(2,1)}, bf16[128,1408]{1,0:T(8,128)(2,1)}, u32[]{:S(2)}, u32[]{:S(2)}) collective-permute-start(bf16[128,1408]{1,0:T(8,128)(2,1)} %collective-permute-done.16), channel_id=1, source_target_pairs={{0,256},{16,272},{32,288},{48,304},{64,320},{80,336},{96,352},{112... | collective-permute-start | bytes 1081352 | tf_op jit(solution)/shard_map/ppermute | solution.py:13
  731.2 1.2 copy-start.20
  732.6 13.9 %copy-start.23 = (f32[128,384]{1,0:T(8,128)S(1)}, f32[128,384]{1,0:T(8,128)}, u32[]{:S(2)}) copy-start(f32[128,384]{1,0:T(8,128)} %get-tuple-element.34) | copy-start | bytes 589828
  732.6 13.9 %copy-start.38 = (bf16[1,384,1408]{2,1,0:T(8,128)(2,1)S(1)}, bf16[1,384,1408]{2,1,0:T(8,128)(2,1)}, u32[]{:S(2)}) copy-start(bf16[1,384,1408]{2,1,0:T(8,128)(2,1)} %all-gather.4.cloned.1.call-done) | copy-start | bytes 3244036
  745.8 0.7 copy-start.16
  747.6 1.4 copy-start.5
  747.6 1.4 copy-start.11
  748.9 126.6 %reduce-scatter.12.cloned.1.call-start = ((), (), s32[]{:S(2)}) async-start(), calls=%async_computation.15 | async-start | bytes 1622016
  758.7 0.9 copy-start.33
  758.8 150.5 %reduce-scatter.10.cloned.1.call-start = ((), (), s32[]{:S(2)}) async-start(), calls=%async_computation.14 | async-start | bytes 1486848
  761.5 74.4 %copy-start.17 = (bf16[128,1408]{1,0:T(8,128)(2,1)S(1)}, bf16[128,1408]{1,0:T(8,128)(2,1)}, u32[]{:S(2)}) copy-start(bf16[128,1408]{1,0:T(8,128)(2,1)} %copy-done.16) | copy-start | bytes 1081348
  763.9 74.0 %copy-start.3 = (bf16[128,1408]{1,0:T(8,128)(2,1)S(1)}, bf16[128,1408]{1,0:T(8,128)(2,1)}, u32[]{:S(2)}) copy-start(bf16[128,1408]{1,0:T(8,128)(2,1)} %copy-done.2) | copy-start | bytes 1081348
  763.9 74.0 %copy-start.9 = (bf16[128,1408]{1,0:T(8,128)(2,1)S(1)}, bf16[128,1408]{1,0:T(8,128)(2,1)}, u32[]{:S(2)}) copy-start(bf16[128,1408]{1,0:T(8,128)(2,1)} %copy-done.8) | copy-start | bytes 1081348
  763.9 74.0 %copy-start.15 = (bf16[128,1408]{1,0:T(8,128)(2,1)S(1)}, bf16[128,1408]{1,0:T(8,128)(2,1)}, u32[]{:S(2)}) copy-start(bf16[128,1408]{1,0:T(8,128)(2,1)} %copy-done.14) | copy-start | bytes 1081348
  764.7 73.2 %copy-start.29 = (bf16[128,2,176]{0,2,1:T(8,128)(2,1)S(1)}, bf16[128,2,176]{0,2,1:T(8,128)(2,1)}, u32[]{:S(2)}) copy-start(bf16[128,2,176]{0,2,1:T(8,128)(2,1)} %get-tuple-element.29) | copy-start | bytes 270340
  764.7 73.2 %copy-start.30 = (bf16[128,2,176]{0,2,1:T(8,128)(2,1)S(1)}, bf16[128,2,176]{0,2,1:T(8,128)(2,1)}, u32[]{:S(2)}) copy-start(bf16[128,2,176]{0,2,1:T(8,128)(2,1)} %get-tuple-element.30) | copy-start | bytes 270340
  764.7 73.2 %copy-start.31 = (bf16[128,2,176]{0,2,1:T(8,128)(2,1)S(1)}, bf16[128,2,176]{0,2,1:T(8,128)(2,1)}, u32[]{:S(2)}) copy-start(bf16[128,2,176]{0,2,1:T(8,128)(2,1)} %get-tuple-element.31) | copy-start | bytes 270340
  764.7 73.2 %copy-start.32 = (bf16[128,2,176]{0,2,1:T(8,128)(2,1)S(1)}, bf16[128,2,176]{0,2,1:T(8,128)(2,1)}, u32[]{:S(2)}) copy-start(bf16[128,2,176]{0,2,1:T(8,128)(2,1)} %get-tuple-element.32) | copy-start | bytes 270340
  837.1 0.7 copy-start.18
  839.4 1.1 copy-start.7
  839.4 1.3 copy-start.13
  840.5 103.9 %reduce-scatter.8.cloned.1.call-start = ((), (), s32[]{:S(2)}) async-start(), calls=%async_computation.13 | async-start | bytes 1622016 | tf_op jit(solution)/shard_map/reduce_scatter | solution.py:121
  843.7 1.0 copy-start.19
  (4 other events, 2.6 us)
Sparse Core Ops, SparseCore 0:
  10.1 39.1 all-gather.5
  51.4 33.3 all-gather.3
  88.0 85.4 all-reduce.4
  183.0 48.8 all-gather.7
  307.7 86.5 all-reduce.6
  527.9 86.9 all-reduce.8
  749.0 86.8 all-reduce.10
  838.7 36.7 reduce-scatter.11
  878.3 30.8 reduce-scatter.9
  912.5 31.8 reduce-scatter.7
